TPU v7x, 32 devices: a whole 2x2x4 slice. The times are simulated.
32 devices in a mesh: dp: 4 (over y, core), fsdp: 8 (over z, x).
Axes of the slice: x: 2, y: 2, z: 4, core: 2. Of those that a mesh axis runs over, the one named last changes fastest.
Arguments:
- patches: bfloat16 [32, 768, 768], P(('dp', 'fsdp')), may hold values from -6 to 6
- positions: int32 [32, 768], P(('dp', 'fsdp')), may hold values from 0 to 198, as said below
- segments: int32 [32, 768], P(('dp', 'fsdp')), may hold values from 0 to 15, as said below
- labels: int32 [32, 15], P(('dp', 'fsdp')), may hold values from 0 to 999
- teacher: int32 [32, 15], P(('dp', 'fsdp')), may hold values from 0 to 999
- layer_master: float32 [2, 1802240], P(None, ('dp', 'fsdp'))
- layer_moment: float32 [2, 1802240], P(None, ('dp', 'fsdp'))
- layer_second: float32 [2, 1802240], P(None, ('dp', 'fsdp'))
- global_master: float32 [1146880], P(('dp', 'fsdp'))
- global_moment: float32 [1146880], P(('dp', 'fsdp'))
- global_second: float32 [1146880], P(('dp', 'fsdp'))
Outputs:
- new_layer_master: float32 [2, 1802240], P(None, ('dp', 'fsdp'))
- new_layer_moment: float32 [2, 1802240], P(None, ('dp', 'fsdp'))
- new_layer_second: float32 [2, 1802240], P(None, ('dp', 'fsdp'))
- new_global_master: float32 [1146880], P(('dp', 'fsdp'))
- new_global_moment: float32 [1146880], P(('dp', 'fsdp'))
- new_global_second: float32 [1146880], P(('dp', 'fsdp'))
- grad_norm: float32 [], replicated
- loss_sum: float32 [], replicated
Inputs may be any that keep to these rules, and one draw needn't show every extreme that they name: `positions`: in each sequence 15 images of 51 tokens stand in order, with the remaining tokens as padding before, between or after them; an image's first token has position 196, its second 196 + 1, the others rows of the 14 x 14 table in a 7 x 7 window, row by row; padding has position 198. `segments`: the number of a token's image in its sequence, counting from 0 in order; padding tokens have 15.
All inputs are finite; a program needn't handle non-finite values.
Results may differ from a plain program's by a relative error of at most 0.012.
Values may be sent and summed in bfloat16 or wider, within the bound.
A program may use at most 192 MiB of HBM per device.

v0:
```python
import functools

import jax
import jax.numpy as jnp
from jax import lax
from jax.experimental import pallas as pl
from jax.experimental.pallas import tpu as pltpu
from jax.sharding import PartitionSpec as P

D = 384
HEADS = 6
HEAD_DIM = 64
FF = 1536
CLASSES = 1000
PATCH = 768
TABLE = 196
IMAGES = 15
SEQ = 768
STEP = 10
LANES = 128

NORM_EPS = 1e-06
BETA_ONE = 0.9
BETA_TWO = 0.999
ADAM_EPS = 1e-08
LEARN_RATE = 0.1
WEIGHT_DECAY = 0.05
CLIP_NORM = 0.01
MASK_FILL = -1000000000.0
SCORE_SCALE = HEAD_DIM ** (-0.5)
LOW = jnp.bfloat16
FULL = jnp.float32
HIGHEST = lax.Precision.HIGHEST

QKV_AT, PROJ_AT, FC1_AT, FC2_AT = 0, 3456, 4608, 9216
PRE_GAIN_AT, PRE_BIAS_AT, QUERY_BIAS_AT, VALUE_BIAS_AT = 13824, 13827, 13830, 13833
PROJ_BIAS_AT, MID_GAIN_AT, MID_BIAS_AT, FC1_BIAS_AT, FC2_BIAS_AT = 13836, 13839, 13842, 13845, 13857
LAYER_END = 13860
PATCH_AT, POS_AT, PATCH_BIAS_AT, FINAL_GAIN_AT, FINAL_BIAS_AT = 0, 2304, 2898, 2901, 2904
HEAD_AT, HEAD_BIAS_AT, GLOBAL_END = 2907, 8907, 8923
GROUP, GROUP_ROWS, GROUPS = 8, 125, 48
HEAD_LANES = 2048
PICKED = 32
WINDOWS, WINDOW = 8, 128
ROWS = 256
LAYER_ALL, GLOBAL_ALL = 14080, 8960
VMEM_BYTES = 64 * 1024 * 1024 - 64 * 1024
MESH = pl.DeviceIdType.MESH


def dot(a, b, dims=(1, 0), precision=None):
    return lax.dot_general(
        a, b, (((dims[0],), (dims[1],)), ((), ())), precision=precision, preferred_element_type=FULL
    )


def dot_nt(a, b, precision=None):
    return dot(a, b, (1, 1), precision)


def dot_tn(a, b, precision=None):
    return dot(a, b, (0, 0), precision)


def row_mean(x):
    return jnp.sum(x, axis=-1, keepdims=True) * (1.0 / D)


def normalise(x):
    center = x - row_mean(x)
    inverse = lax.rsqrt(row_mean(center * center) + NORM_EPS)
    return center * inverse, inverse


def norm_back(grad, gain, unit, inverse):
    scaled = grad * gain
    return inverse * (scaled - row_mean(scaled) - unit * row_mean(scaled * unit))


def col_sum(x):
    return jnp.sum(x.astype(FULL), axis=0, keepdims=True)


def gelu_parts(x):
    size = jnp.abs(x)
    bell = jnp.exp(-0.5 * x * x)
    base = 1.0 + (0.3275911 * 0.7071067811865476) * size
    t = pl.reciprocal(base, approx=True)
    t = t * (2.0 - base * t)
    tail = ((((1.061405429 * t - 1.453152027) * t + 1.421413741) * t - 0.284496736) * t + 0.254829592) * t
    tail = 0.5 * tail * bell
    phi = jnp.where(x < 0, tail, 1.0 - tail)
    return x * phi, phi + x * (bell * 0.3989422804014327)


def exact_parts(x):
    high = x.astype(LOW)
    rest = x - high.astype(FULL)
    middle = rest.astype(LOW)
    return high, middle, (rest - middle.astype(FULL)).astype(LOW)


def wrap(value, size):
    return jnp.where(value >= size, value - size, value)


class Place:
    def __init__(self, sizes):
        dp, fsdp = sizes
        self.n = self.ny = self.nx = dp // 2
        self.nz = fsdp // self.nx
        assert dp == 2 * self.n and fsdp == self.n * self.nz

    def locate(self):
        dp, fsdp = lax.axis_index("dp"), lax.axis_index("fsdp")
        self.y, self.core = dp // 2, dp % 2
        self.z, self.x = fsdp // self.nx, fsdp % self.nx
        self.even = self.core == 0
        self.zs = [wrap(self.z + k, self.nz) for k in range(self.nz)]
        self.ys = [wrap(self.y + k, self.n) for k in range(self.n)]
        self.xs = [wrap(self.x + k, self.n) for k in range(self.n)]
        spans = [(p, q) for p in range(self.n) for q in range(self.n)]
        self.short = {
            (p, q): (jnp.where(self.even, self.ys[p], self.ys[q]), jnp.where(self.even, self.xs[q], self.xs[p]))
            for p, q in spans
        }

    def yx(self, p, q):
        return self.short[p, q]

    def block(self, dz, p, q):
        y, x = self.yx(p, q)
        return y, self.core, self.zs[dz], x

    def device(self, y, core, z, x):
        return y * 2 + core, z * self.nx + x

    def yx_other(self, p, q):
        return jnp.where(self.even, self.ys[q], self.ys[p]), jnp.where(self.even, self.xs[p], self.xs[q])

    def index(self, y, core, z, x):
        return ((y * 2 + core) * self.nz + z) * self.nx + x

    def meet(self):
        def there(y=0, core=0, z=0, x=0):
            return self.device(self.ys[y], 1 - self.core if core else self.core, self.zs[z], self.xs[x])

        self.other = there(core=1)
        self.zp = [there(z=k) for k in range(self.nz)]
        self.pp = [self.device(*self.block(0, k, 0)) for k in range(self.n)]
        self.qp = [self.device(*self.block(0, 0, k)) for k in range(self.n)]
        self.tall = [there(core=c, z=k) for c in range(2) for k in range(self.nz)][1:]
        self.flat = [there(y=j, x=k) for j in range(self.n) for k in range(self.n)][1:]
        barrier = pltpu.get_barrier_semaphore()
        for peer in self.tall + self.flat:
            pl.semaphore_signal(barrier, inc=1, device_id=peer, device_id_type=MESH)
        pl.semaphore_wait(barrier, len(self.tall + self.flat))


def push(src, dst, send, recv, peer):
    pltpu.make_async_remote_copy(
        src_ref=src, dst_ref=dst, send_sem=send, recv_sem=recv, device_id=peer, device_id_type=MESH
    ).start()


def landed(dst, recv):
    pltpu.make_async_copy(dst, dst, recv).wait()


class Plan:
    HOP = 2.5
    RATES = (88e3, 66e3, 600e3)

    def __init__(self):
        self.now, self.free, self.came, self.steps = 0.0, [0.0] * 3, {}, []

    def sent(self, key, way, size):
        begin = max(self.now, self.free[way])
        self.free[way] = begin + size / self.RATES[way]
        self.came[key] = max(self.came.get(key, 0.0), self.free[way] + self.HOP)

    def add(self, needs, run, name=None):
        self.steps.append((needs, run, name))

    def ready(self, step):
        return max((self.came.get(key, 1e9) for key in step[0]), default=0.0)

    def run(self, step):
        self.steps.remove(step)
        self.now = max(self.now, self.ready(step)) + 0.03
        step[1]()

    def spend(self, time):
        self.now += time
        while True:
            step = next((step for step in self.steps if self.ready(step) <= self.now), None)
            if step is None:
                return
            self.run(step)

    def until(self, name=None):
        while self.steps and (name is None or any(step[2] == name for step in self.steps)):
            self.run(min(self.steps, key=self.ready))


class Gather:
    def __init__(self, place, plan, name, buf, send, recv):
        self.place, self.plan, self.name, self.buf, self.send, self.recv = place, plan, name, buf, send, recv
        self.from_p = place.nz
        self.from_q = self.from_p + place.nz * place.n
        self.from_core = self.from_q + place.n
        self.size = 2 * buf.shape[4] * LANES

    def sent(self, way, count, *key):
        self.plan.sent((self.name,) + key, way, count * self.size)

    def to_p(self, dz):
        a, t = self.place, self.buf.at[self.place.block(dz, 0, 0)]
        for k in range(1, a.n):
            push(t, t, self.send, self.recv.at[self.from_p + dz * a.n + a.n - k], a.pp[k])
            self.sent(0, 1, 1, dz, a.n - k)

    def to_q(self, dz, p):
        a, t = self.place, self.buf.at[self.place.block(dz, p, 0)]
        for k in range(1, a.n):
            push(t, t, self.send, self.recv.at[self.from_q + a.n - k], a.qp[k])
            self.sent(0, 1, 2, dz, p)

    def start(self):
        a, t = self.place, self.buf.at[self.place.block(0, 0, 0)]
        self.to_p(0)
        for k in range(1, a.nz):
            push(t, t, self.send, self.recv.at[a.nz - k], a.zp[k])
            self.sent(1, 1, 0, a.nz - k)
        self.to_q(0, 0)
        far = range(1, a.n)
        near = sorted(range(1, a.nz), key=lambda k: min(k, a.nz - k))
        add = self.plan.add
        for p in far:
            add([(self.name, 1, 0, p)], lambda p=p: self.p_came(0, p))
        for k in near:
            add([(self.name, 0, k)], lambda k=k: self.z_came(k))
        for k in near:
            for p in far:
                add([(self.name, 1, k, p)], lambda k=k, p=p: self.p_came(k, p))
        mine = [(self.name, 0, k) for k in near] + [(self.name, 1, k, p) for k in range(a.nz) for p in far]
        add(mine, lambda: self.to_core(0))
        for q in far:
            add([(self.name, 2, k, p) for k in range(a.nz) for p in range(a.n)], lambda q=q: self.q_came(q))
        add([(self.name, 3, q) for q in range(a.n)], self.finish, self.name)

    def z_came(self, dz):
        landed(self.buf.at[self.place.block(dz, 0, 0)], self.recv.at[dz])
        self.to_p(dz)
        self.to_q(dz, 0)

    def p_came(self, dz, p):
        landed(self.buf.at[self.place.block(dz, p, 0)], self.recv.at[self.from_p + dz * self.place.n + p])
        self.to_q(dz, p)

    def group(self, core, q):
        a = self.place
        return self.buf.at[:, 0, :, a.xs[q]] if core == 0 else self.buf.at[a.ys[q], 1]

    def to_core(self, q):
        a = self.place
        for core in range(2):

            @pl.when(a.core == core)
            def _():
                t = self.group(core, q)
                push(t, t, self.send, self.recv.at[self.from_core + q], a.other)

        self.sent(2, a.n * a.nz, 3, q)

    def q_came(self, q):
        landed(self.buf.at[:, 0, :, 0], self.recv.at[self.from_q + q])
        self.to_core(q)

    def finish(self):
        for q in range(self.place.n):
            landed(self.buf.at[:, 0, :, 0], self.recv.at[self.from_core + q])

    def drain(self):
        a = self.place
        for t in (self.buf.at[:, 0], self.buf.at[:, 0, :, pl.ds(0, a.n - 1)], self.buf.at[0, 0, :, pl.ds(0, a.n - 1)]):
            landed(t, self.send)
        landed(self.buf.at[0, 0, pl.ds(0, a.nz - 1), 0], self.send)


class Scatter:
    def __init__(self, place, plan, buf, from_core, from_q, from_p, from_z, out, send, recv, shares, turn_of):
        self.place, self.plan, self.buf, self.out, self.send, self.recv = place, plan, buf, out, send, recv
        self.core_buf, self.q_buf, self.p_buf, self.z_buf = from_core, from_q, from_p, from_z
        self.shares, self.turn_of = shares, turn_of
        n, nz = place.n, place.nz
        self.at_q = n * n * nz
        self.at_p = self.at_q + n * n * nz
        self.at_z = self.at_p + n * nz
        self.past = []
        self.far = tuple(range(1, n))
        self.order = sorted(range(1, nz), key=lambda k: -min(k, nz - k)) + [0]
        self.size = 2 * buf.shape[4] * LANES

    def when(self, turn, block, body):
        pl.when(self.turn_of(self.place.index(*block)) == turn)(body)

    def send_on(self, turn, block, src, dst, recv, peer):
        push(src, dst, self.send, recv, peer)
        self.past.append((turn, block, src))

    def sent(self, turn, way, *key):
        self.plan.sent((id(self), turn) + key, way, self.size * self.shares[turn])

    def block(self, p, q, k):
        y, x = self.place.yx(p, q)
        return y, self.place.core, self.place.zs[k], x

    def start(self, turn):
        a, name = self.place, (id(self), turn)
        for k in self.order:
            for q in self.far + (0,):
                for p in self.far + (0,):
                    y, x = a.yx_other(p, q)
                    z = a.zs[k]
                    block = y, 1 - a.core, z, x
                    recv = self.recv.at[(q * a.n + p) * a.nz + k]
                    self.when(turn, block, lambda: self.send_on(
                        turn, block, self.buf.at[block], self.core_buf.at[y, z, x], recv, a.other))
                    self.sent(turn, 2, 0, p, q, k)
        add = self.plan.add
        for k in self.order:
            for q in self.far:
                for p in self.far + (0,):
                    add([name + (0, p, q, k)], lambda p=p, q=q, k=k: self.to_q(turn, p, q, k))

            def needs(p):
                return [name + (0, p, 0, k)] + [name + (1, p, q, k) for q in self.far]

            for p in self.far:
                add(needs(p), lambda p=p, k=k: self.to_p(turn, p, k))
            here = needs(0) + [name + (2, p, k) for p in self.far]
            if k:
                add(here, lambda k=k: self.to_z(turn, k))
            else:
                add(here + [name + (3, j) for j in range(1, a.nz)], lambda: self.own(turn))

    def add(self, p, q, k, extra, out=None):
        a = self.place
        y, core, z, x = self.block(p, q, k)
        mine, theirs = self.buf.at[y, core, z, x], self.core_buf.at[y, z, x]
        landed(theirs, self.recv.at[(q * a.n + p) * a.nz + k])
        refs = [mine, theirs] + extra
        if out is None:
            add_up(refs, mine)
        else:
            out(refs)
        return mine

    def to_q(self, turn, p, q, k):
        a = self.place
        block = self.block(p, q, k)

        def body():
            mine = self.add(p, q, k, [])
            recv = self.recv.at[self.at_q + ((a.n - q) * a.n + p) * a.nz + k]
            self.send_on(turn, block, mine, self.q_buf.at[a.n - q - 1, p, a.zs[k]], recv, a.qp[q])

        self.when(turn, block, body)
        self.sent(turn, 0, 1, p, a.n - q, k)

    def q_came(self, p, k):
        a = self.place
        refs = [self.q_buf.at[q - 1, p, a.zs[k]] for q in self.far]
        for q, ref in zip(self.far, refs):
            landed(ref, self.recv.at[self.at_q + (q * a.n + p) * a.nz + k])
        return refs

    def to_p(self, turn, p, k):
        a = self.place
        block = self.block(p, 0, k)

        def body():
            mine = self.add(p, 0, k, self.q_came(p, k))
            recv = self.recv.at[self.at_p + (a.n - p) * a.nz + k]
            self.send_on(turn, block, mine, self.p_buf.at[a.n - p - 1, a.zs[k]], recv, a.pp[p])

        self.when(turn, block, body)
        self.sent(turn, 0, 2, a.n - p, k)

    def p_came(self, k):
        a = self.place
        refs = [self.p_buf.at[p - 1, a.zs[k]] for p in self.far]
        for p, ref in zip(self.far, refs):
            landed(ref, self.recv.at[self.at_p + p * a.nz + k])
        return refs

    def to_z(self, turn, k):
        a = self.place
        block = self.block(0, 0, k)

        def body():
            mine = self.add(0, 0, k, self.q_came(0, k) + self.p_came(k))
            recv = self.recv.at[self.at_z + a.nz - k]
            self.send_on(turn, block, mine, self.z_buf.at[a.nz - k - 1], recv, a.zp[k])

        self.when(turn, block, body)
        self.sent(turn, 1, 3, a.nz - k)

    def own(self, turn):
        a = self.place

        def body():
            extra = self.q_came(0, 0) + self.p_came(0)
            for k in range(1, a.nz):
                landed(self.z_buf.at[k - 1], self.recv.at[self.at_z + k])
            self.add(0, 0, 0, extra + [self.z_buf.at[k] for k in range(a.nz - 1)], self.out)

        self.when(turn, self.block(0, 0, 0), body)

    def drain(self):
        for turn, block, src in self.past:
            self.when(turn, block, lambda: landed(src, self.send))


def sum_rows(refs, r):
    value = refs[0][r, :].astype(FULL)
    for ref in refs[1:]:
        value += ref[r, :].astype(FULL)
    return value


def add_up(refs, dst):
    rows = dst.shape[0]
    step = next(v for v in (224, 144, 64, 48, 32, 16) if rows % v == 0)

    def one(t, carry):
        r = pl.ds(pl.multiple_of(t * step, step), step)
        dst[r, :] = sum_rows(refs, r).astype(LOW)
        return carry

    lax.fori_loop(0, rows // step, one, 0)


def add_over_slice(place, tile, tiles, send, recv):
    base = 0
    for turn, (peers, own) in enumerate((
        (place.tall, place.core * place.nz + place.z), (place.flat, place.y * place.n + place.x)
    )):
        mine = tiles.at[base + own]
        mine[...] = tile
        for peer in peers:
            push(mine, mine, send.at[turn], recv.at[turn], peer)
        landed(tiles.at[pl.ds(base, len(peers))], recv.at[turn])
        tile = tiles[base]
        for k in range(1, len(peers) + 1):
            tile += tiles[base + k]
        landed(tiles.at[pl.ds(base, len(peers))], send.at[turn])
        base += len(peers) + 1
    return tile


def step_kernel(
    place, loss_scale,
    pat, pos, seg, lab, tea, lm, gm,
    new_l, new_g, shared,
    b0, b1, bg, r0c, r0q, r0p, r0z, r1c, r1q, r1p, r1z, rgc, rgq, rgp, rgz, flat, edge, stage, arrange,
    wqkv, wproj, wfc1, wfc2, wpat, wpos, whead, vecs,
    pos_col, seg_col, unit_a, inv_a, h_a, unit_b, inv_b, h_b, qkv, probs, attl, x0, x1, slope, act, kv, low, inv_c,
    tiles, sends, gather_recv, scatter_recv, tile_send, tile_recv,
):
    layer_rows, global_rows = lm.shape[0] // 2, gm.shape[0]
    place.locate()
    me = place.block(0, 0, 0)
    bg[me + (pl.ds(0, global_rows),)] = gm[...].astype(LOW)
    b0[me + (pl.ds(0, layer_rows),)] = lm[pl.ds(0, layer_rows, stride=2), :].astype(LOW)
    b1[me + (pl.ds(0, layer_rows),)] = lm[pl.ds(1, layer_rows, stride=2), :].astype(LOW)
    place.meet()
    plan = Plan()
    gathers = [
        Gather(place, plan, i, buf, sends.at[i], gather_recv.at[i]) for i, buf in enumerate((bg, b0, b1))
    ]
    gathers[0].start()
    gathers[1].start()

    def split_rows(rows):
        half = rows // 32 * 16
        return [pl.ds(at, count) for at, count in ((0, half), (half, rows - half)) if count]

    def finish_layer(n):
        def out(refs):
            for r in split_rows(layer_rows):
                new_l[pl.ds(2 * r.start + n, r.size, stride=2), :] = sum_rows(refs, r)

        return out

    def finish_global(refs):
        for r in split_rows(global_rows):
            new_g[r, :] = sum_rows(refs, r)

    def layer_turn(s):
        first, last = PRE_GAIN_AT // layer_rows, (PROJ_BIAS_AT - 1) // layer_rows
        late = (s < -(-PROJ_AT // layer_rows)).astype(jnp.int32)
        return jnp.where((s >= first) & (s <= last), 2, late)

    def global_turn(s):
        return (s < -(-FINAL_GAIN_AT // global_rows)).astype(jnp.int32)

    scatter_g = Scatter(place, plan, bg, rgc, rgq, rgp, rgz, finish_global, sends.at[5], scatter_recv.at[2],
                        (0.7, 0.5), global_turn)
    scatter_0 = Scatter(place, plan, b0, r0c, r0q, r0p, r0z, finish_layer(0), sends.at[4], scatter_recv.at[1],
                        (0.9, 0.5, 0.05), layer_turn)
    scatter_1 = Scatter(place, plan, b1, r1c, r1q, r1p, r1z, finish_layer(1), sends.at[3], scatter_recv.at[0],
                        (1.0,), lambda s: 0 * s)
    scatters = [scatter_g, scatter_0, scatter_1]
    first_early = -(-PROJ_AT // layer_rows)
    vector_blocks = PRE_GAIN_AT // layer_rows, (PROJ_BIAS_AT - 1) // layer_rows + 1

    head_of_lane = lax.broadcasted_iota(jnp.int32, (1, LANES), 1) // HEAD_DIM

    def loop(count, body, carry=None, time=0.0):
        for i in range(count):
            carry = body(i, carry)
            plan.spend(time)
        return carry

    def rolled(count, body, carry=None, time=0.0):
        carry = lax.fori_loop(0, count, body, 0 if carry is None else carry)
        plan.spend(time)
        return carry

    def each_block(low_end, high_end, one):
        def body(s, carry):
            x = lax.rem(s, place.nx)
            rest = lax.div(s, place.nx)
            z, rest = lax.rem(rest, place.nz), lax.div(rest, place.nz)
            one(s, (lax.div(rest, 2), lax.rem(rest, 2), z, x))
            return carry

        lax.fori_loop(low_end, high_end, body, 0)

    def spread(buf, rows, low_end=0, high_end=2 * place.n * place.n * place.nz):
        def one(s, t):
            if rows % 8 == 0:
                flat[pl.ds(pl.multiple_of(s * rows, 8), rows), :] = buf[t + (pl.ds(0, rows),)].astype(FULL)
            else:
                stage[: buf.shape[4], :] = buf[t].astype(FULL)

                def row(i, carry):
                    flat[pl.ds(s * rows + i, 1), :] = stage[pl.ds(i, 1), :]
                    return carry

                lax.fori_loop(0, rows, row, 0)

        each_block(low_end, high_end, one)

    def gather_rows(buf, rows, low_end=0, high_end=2 * place.n * place.n * place.nz):
        def one(s, t):
            if rows % 8 == 0:
                buf[t + (pl.ds(0, rows),)] = flat[pl.ds(pl.multiple_of(s * rows, 8), rows), :].astype(LOW)
            else:

                def row(i, carry):
                    stage[pl.ds(i, 1), :] = flat[pl.ds(s * rows + i, 1), :]
                    return carry

                lax.fori_loop(0, rows, row, 0)
                buf[t] = stage[: buf.shape[4], :].astype(LOW)

        each_block(low_end, high_end, one)

    def take(dst, at, rows, width):
        count = width // LANES

        def one(c, carry):
            value = flat[pl.ds(at + c, rows, stride=count), :].astype(LOW)
            dst[:rows, pl.ds(pl.multiple_of(c * LANES, LANES), LANES)] = value
            return carry

        lax.fori_loop(0, count, one, 0)

    def take_row(at, width):
        return jnp.concatenate([flat[at + i : at + i + 1, :] for i in range(width // LANES)], axis=1)

    def put_row(at, value):
        for i in range(value.shape[1] // LANES):
            flat[at + i : at + i + 1, :] = value[:, i * LANES : (i + 1) * LANES]

    def put(at, start, width, value, first=0):
        count = width // LANES
        rows = value.shape[0]
        for i in range(value.shape[1] // LANES):
            flat[pl.ds(at + start * count + first + i, rows, stride=count), :] = value[:, i * LANES : (i + 1) * LANES]

    for i in range(SEQ // LANES):
        lanes = slice(i * LANES, (i + 1) * LANES)
        for src, dst in ((pos, pos_col), (seg, seg_col)):
            dst[lanes, :] = jnp.transpose(jnp.broadcast_to(src[0:1, lanes].astype(FULL), (LANES, LANES)))
    pos_row = pos[0:1, :]
    seg_row = seg[0:1, :]
    picked_row = lax.broadcasted_iota(jnp.int32, (PICKED, 1), 0)
    picked_image = jnp.where(picked_row < IMAGES, picked_row, picked_row - IMAGES)
    picked_image = jnp.where(picked_row < 2 * IMAGES, picked_image, -1)
    picked_place = jnp.where(picked_row < IMAGES, TABLE, TABLE + 1)
    picker = ((seg_row == picked_image) & (pos_row == picked_place)).astype(FULL)
    picker_low = picker.astype(LOW)

    arr_row = lax.broadcasted_iota(jnp.int32, (D, GROUP * LANES), 0)
    arr_lane = lax.broadcasted_iota(jnp.int32, (D, GROUP * LANES), 1)
    arrange[...] = (
        (arr_row == (arr_lane % LANES) * GROUP + arr_lane // LANES) & (arr_lane % LANES < GROUPS)
    ).astype(FULL).astype(LOW)

    plan.spend(1.0)
    plan.until(0)
    gathers[2].start()
    spread(bg, global_rows)
    plan.spend(1.2)
    take(wpat, PATCH_AT, PATCH, D)
    take(wpos, POS_AT, TABLE + 2, D)
    wpos[TABLE + 2 :, :] = jnp.zeros((wpos.shape[0] - TABLE - 2, D), LOW)

    def take_head(j, carry):
        value = flat[pl.ds(HEAD_AT + j, GROUPS, stride=GROUP_ROWS), :].astype(LOW)
        whead[:, pl.ds(pl.multiple_of(j * LANES, LANES), LANES)] = value
        return carry

    lax.fori_loop(0, GROUP_ROWS, take_head, 0)
    whead[:, GROUP_ROWS * LANES :] = jnp.zeros((GROUPS, LANES), LOW)
    patch_bias = take_row(PATCH_BIAS_AT, D)
    final_gain = take_row(FINAL_GAIN_AT, D)
    final_bias = take_row(FINAL_BIAS_AT, D)
    head_bias = take_row(HEAD_BIAS_AT, HEAD_LANES)

    row_at = (
        (PRE_GAIN_AT, D), (PRE_BIAS_AT, D), (QUERY_BIAS_AT, D), (VALUE_BIAS_AT, D), (PROJ_BIAS_AT, D),
        (MID_GAIN_AT, D), (MID_BIAS_AT, D), (FC1_BIAS_AT, FF), (FC2_BIAS_AT, D),
    )

    def take_layer(n, buf):
        spread(buf, layer_rows)
        take(wqkv.at[n], QKV_AT, D, 3 * D)
        take(wproj.at[n], PROJ_AT, D, D)
        take(wfc1.at[n], FC1_AT, D, FF)
        take(wfc2.at[n], FC2_AT, FF, D)
        for i, (at, width) in enumerate(row_at):
            vecs[n, i : i + 1, :width] = take_row(at, width)

    def vec(n, i):
        return vecs[n, i : i + 1, : row_at[i][1]]

    plan.spend(2.0)

    def tile_rows(i):
        return pl.ds(pl.multiple_of(i * ROWS, ROWS), ROWS)

    def onehot_of(place):
        iota = lax.broadcasted_iota(jnp.int32, (1, wpos.shape[0]), 1).astype(FULL)
        return (place == iota).astype(LOW)

    def embed(i, carry):
        r = tile_rows(i)
        place = pos_col[r, 0:1]
        pixel = dot(pat[r, :], wpat[...]) + patch_bias
        stream = dot(onehot_of(place), wpos[...]) + jnp.where(place < TABLE, pixel, 0.0)
        x0[r, :] = stream
        unit, inverse = normalise(stream)
        unit_a[r, :] = unit
        inv_a[r, :] = jnp.broadcast_to(inverse, (ROWS, LANES))
        return carry

    rolled(SEQ // ROWS, embed, None, 1.8)
    plan.until(1)
    take_layer(0, b0)
    plan.spend(1.8)
    qkv_bias = jnp.concatenate([vec(0, 2), jnp.zeros((1, D), FULL), vec(0, 3)], axis=1)

    def project(i, carry):
        r = tile_rows(i)
        h = (unit_a[r, :] * vec(0, 0) + vec(0, 1)).astype(LOW)
        h_a[r, :] = h
        qkv[r, :] = (dot(h, wqkv[0]) + qkv_bias).astype(LOW)
        return carry

    rolled(SEQ // ROWS, project, None, 1.2)

    def window_rows(j):
        return pl.ds(min(102 * j // 16 * 16, SEQ - WINDOW), WINDOW)

    def both(x):
        zero = jnp.zeros_like(x)
        return jnp.concatenate([jnp.where(head_of_lane == 0, x, zero), jnp.where(head_of_lane == 1, x, zero)], axis=0)

    def merge(x):
        return jnp.where(head_of_lane == 0, x[:WINDOW], x[WINDOW:])

    attl[...] = jnp.zeros_like(attl)

    def window_masks(j, r):
        own = seg_col[r, :]
        first = 2.0 * j
        mine = (own >= first) & (own < first + 2.0)
        other = jnp.transpose(jnp.where(mine, own, -1.0))
        pair = jnp.concatenate([own, own], axis=1) == jnp.concatenate([other, other], axis=1)
        return mine, pair

    def keep_own(mine, ref, r, lanes, value):
        ref[r, lanes] = jnp.where(mine, value, ref[r, lanes].astype(FULL)).astype(LOW)

    def attend(j, carry):
        r = window_rows(j)
        mine, pair = window_masks(j, r)
        for g in range(HEADS // 2):
            lanes = slice(g * LANES, (g + 1) * LANES)
            q2 = both(qkv[r, lanes])
            keys = qkv[r, D + g * LANES : D + (g + 1) * LANES]
            values = qkv[r, 2 * D + g * LANES : 2 * D + (g + 1) * LANES]
            scores = jnp.where(pair, dot_nt(keys, q2) * SCORE_SCALE, MASK_FILL)
            e = jnp.exp(scores - jnp.max(scores, axis=0, keepdims=True))
            p = jnp.where(pair, e * (1.0 / jnp.sum(e, axis=0, keepdims=True)), 0.0).astype(LOW)
            probs[j, g] = p
            keep_own(mine, attl, r, lanes, merge(dot_tn(p, values)))
        return carry

    loop(WINDOWS, attend, None, 0.28)

    def feed(i, carry):
        r = tile_rows(i)
        middle = x0[r, :] + dot(attl[r, :], wproj[0]) + vec(0, 4)
        unit, inverse = normalise(middle)
        unit_b[r, :] = unit
        inv_b[r, :] = jnp.broadcast_to(inverse, (ROWS, LANES))
        h = (unit * vec(0, 5) + vec(0, 6)).astype(LOW)
        h_b[r, :] = h
        for c in range(4):
            lanes = slice(c * D, (c + 1) * D)
            value, steep = gelu_parts(dot(h, wfc1[0, :, lanes]) + vecs[0, 7:8, lanes])
            act[r, lanes] = value.astype(LOW)
            slope[r, lanes] = steep.astype(LOW)
        x1[r, :] = middle + dot(act[r, :], wfc2[0]) + vec(0, 8)
        return carry

    rolled(SEQ // ROWS, feed, None, 8.0)

    plan.until(2)
    take_layer(1, b1)
    plan.spend(1.5)
    unit_c = x0
    h_c = low

    def kv_rows(i, carry):
        r = tile_rows(i)
        unit, inverse = normalise(x1[r, :])
        unit_c[r, :] = unit
        inv_c[r, :] = jnp.broadcast_to(inverse, (ROWS, LANES))
        h = (unit * vec(1, 0) + vec(1, 1)).astype(LOW)
        h_c[r, :] = h
        bias = jnp.concatenate([jnp.zeros((1, D), FULL), vec(1, 3)], axis=1)
        kv[r, :] = (dot(h, wqkv[1, :, D:]) + bias).astype(LOW)
        return carry

    rolled(SEQ // ROWS, kv_rows, None, 1.2)

    h_s = dot(picker_low, h_c[...]).astype(LOW)
    x_s = sum(dot(picker_low, part) for part in exact_parts(x1[...]))
    q_s = (dot(h_s, wqkv[1, :, :D]) + vec(1, 2)).astype(LOW)
    stack_rows = lax.broadcasted_iota(jnp.int32, (HEADS * PICKED, 1), 0)
    stack_lanes = lax.broadcasted_iota(jnp.int32, (1, D), 1)
    own_head = (stack_rows // PICKED) == (stack_lanes // HEAD_DIM)

    def stack(x):
        tall = jnp.concatenate([x.astype(FULL)] * HEADS, axis=0)
        return jnp.where(own_head, tall, 0.0).astype(LOW)

    def unstack(x):
        x = jnp.where(own_head, x, 0.0)
        total = x[:PICKED]
        for h in range(1, HEADS):
            total += x[h * PICKED : (h + 1) * PICKED]
        return total

    q6 = stack(q_s)
    image6 = jnp.concatenate([picked_image] * HEADS, axis=0)
    mask6 = image6 == seg_row
    scores = jnp.where(mask6, dot_nt(q6, kv[:, :D]) * SCORE_SCALE, MASK_FILL)
    e = jnp.exp(scores - jnp.max(scores, axis=-1, keepdims=True))
    p6 = e / jnp.sum(e, axis=-1, keepdims=True)
    p6_low = p6.astype(LOW)
    att_s = unstack(dot(p6_low, kv[:, D:])).astype(LOW)
    mid_s = x_s + dot(att_s, wproj[1]) + vec(1, 4)
    unit_m, inv_m = normalise(mid_s)
    h2_s = (unit_m * vec(1, 5) + vec(1, 6)).astype(LOW)
    act_s, steep_s = gelu_parts(dot(h2_s, wfc1[1]) + vec(1, 7))
    act_s = act_s.astype(LOW)
    x2_s = mid_s + dot(act_s, wfc2[1]) + vec(1, 8)

    unit_f, inv_f = normalise(x2_s)
    summary = (unit_f * final_gain + final_bias).astype(LOW)
    arranged = dot(summary, arrange[...]).astype(LOW)
    logits = head_bias
    spans = []
    for k in range(GROUP):
        at = 2 * CLASSES * k
        block, shift = at // LANES, at % LANES
        blocks = (at + 2 * CLASSES - 1) // LANES - block + 1
        spans.append((block, shift, blocks))
        s_k = arranged[:, k * LANES : k * LANES + GROUPS]
        wide = (HEAD_LANES // LANES + 1) * LANES
        part = dot(s_k, whead[:, block * LANES : block * LANES + wide])
        if shift:
            part = pltpu.roll(part, wide - shift, 1)
        logits = logits + part[:, :HEAD_LANES]
    column = lax.broadcasted_iota(jnp.int32, (PICKED, HEAD_LANES), 1)
    second = picked_row >= IMAGES
    low_end = jnp.where(second, CLASSES, 0)
    valid = (column >= low_end) & (column < low_end + CLASSES)
    live = picked_row < 2 * IMAGES
    target = jnp.zeros((PICKED, 1), jnp.int32)
    for i in range(IMAGES):
        target = jnp.where(picked_row == i, lab[0, i], target)
        target = jnp.where(picked_row == IMAGES + i, CLASSES + tea[0, i], target)
    hit = column == target
    logits = jnp.where(valid, logits, -3e38)
    top = jnp.max(logits, axis=-1, keepdims=True)
    e = jnp.exp(logits - top)
    total = jnp.sum(e, axis=-1, keepdims=True)
    hit_logit = jnp.sum(jnp.where(hit, logits, 0.0), axis=-1, keepdims=True)
    each = jnp.where(live, top + jnp.log(total) - hit_logit, 0.0)
    loss_sum = jnp.sum(each, axis=0, keepdims=True)
    grad_logits = jnp.where(live, (e / total - hit.astype(FULL)) * loss_scale, 0.0)
    grad_low = grad_logits.astype(LOW)
    grad_wide = jnp.concatenate([grad_low.astype(FULL), jnp.zeros((PICKED, LANES), FULL)], axis=1)

    grad_arranged = []
    for k, (block, shift, blocks) in enumerate(spans):
        turned = (pltpu.roll(grad_wide, shift, 1) if shift else grad_wide).astype(LOW)
        turned = turned[:, : blocks * LANES]
        s_k = arranged[:, k * LANES : k * LANES + GROUPS]
        grad_w = dot_tn(s_k, turned)
        for j in range(blocks):
            rows = pl.ds(HEAD_AT + block + j, GROUPS, stride=GROUP_ROWS)
            piece = grad_w[:, j * LANES : (j + 1) * LANES]
            if k and j == 0:
                piece = piece + flat[rows, :]
            flat[rows, :] = piece
        back = dot_nt(turned, whead[:, block * LANES : (block + blocks) * LANES])
        grad_arranged.append(jnp.concatenate([back, jnp.zeros((PICKED, LANES - GROUPS), FULL)], axis=1))
    parts = jnp.concatenate(exact_parts(jnp.concatenate(grad_arranged, axis=1)), axis=0)
    parts = dot_nt(parts, arrange[...])
    grad_summary = parts[:PICKED] + parts[PICKED : 2 * PICKED] + parts[2 * PICKED :]
    put_row(HEAD_BIAS_AT, col_sum(grad_low))
    put_row(FINAL_GAIN_AT, col_sum(grad_summary * unit_f))
    put_row(FINAL_BIAS_AT, col_sum(grad_summary))
    flat[GLOBAL_END:GLOBAL_ALL, :] = jnp.zeros((GLOBAL_ALL - GLOBAL_END, LANES), FULL)
    for gather in gathers:
        gather.drain()
    border = FINAL_GAIN_AT // global_rows
    gather_rows(bg, global_rows, border + 1)
    kept = (border + 1) * global_rows - FINAL_GAIN_AT
    edge[:kept, :] = flat[FINAL_GAIN_AT : FINAL_GAIN_AT + kept, :]
    plan.spend(6.0)
    scatter_g.start(0)

    dx_s = norm_back(grad_summary, final_gain, unit_f, inv_f)

    out_s = dx_s.astype(LOW)
    for c in range(4):
        put(FC2_AT, c * D, D, dot_tn(act_s[:, c * D : (c + 1) * D], out_s))
    put_row(FC2_BIAS_AT, col_sum(out_s))
    gpre_s = (dot_nt(out_s, wfc2[1]) * steep_s).astype(LOW)
    put(FC1_AT, 0, FF, dot_tn(h2_s, gpre_s))
    put_row(FC1_BIAS_AT, col_sum(gpre_s))
    gh2_s = dot_nt(gpre_s, wfc1[1])
    put_row(MID_GAIN_AT, col_sum(gh2_s * unit_m))
    put_row(MID_BIAS_AT, col_sum(gh2_s))
    gmid_s = dx_s + norm_back(gh2_s, vec(1, 5), unit_m, inv_m)
    gmid_low = gmid_s.astype(LOW)
    put(PROJ_AT, 0, D, dot_tn(att_s, gmid_low))
    put_row(PROJ_BIAS_AT, col_sum(gmid_low))
    plan.spend(1.0)
    gatt6 = stack(dot_nt(gmid_low, wproj[1]).astype(LOW))
    gprob = dot_nt(gatt6, kv[:, D:])
    gscore = (p6 * (gprob - jnp.sum(p6 * gprob, axis=-1, keepdims=True))).astype(LOW)
    gq_s = (unstack(dot(gscore, kv[:, :D])) * SCORE_SCALE).astype(LOW)
    gkeys = (dot_tn(gscore, q6) * SCORE_SCALE).astype(LOW)
    gvalues = dot_tn(p6_low, gatt6).astype(LOW)
    put_row(QUERY_BIAS_AT, col_sum(gq_s))
    put_row(VALUE_BIAS_AT, col_sum(gvalues))
    kv[:, :D] = gkeys
    kv[:, D:] = gvalues
    plan.spend(2.2)
    put(QKV_AT, 0, 3 * D, dot_tn(h_s, gq_s))
    put(QKV_AT, 0, 3 * D, dot_tn(h_c[...], kv[:, :D]), 3)
    put(QKV_AT, 0, 3 * D, dot_tn(h_c[...], kv[:, D:]), 6)
    back_s = jnp.concatenate([dot_nt(gq_s, wqkv[1, :, :D]), gmid_s], axis=1)

    back_parts = jnp.concatenate(exact_parts(back_s), axis=0)
    dx = x1

    def kv_back(i, carry):
        gain_sum, bias_sum = carry
        r = tile_rows(i)
        image_col = seg_col[r, 0:1]
        place_col = pos_col[r, 0:1]
        lane = lax.broadcasted_iota(jnp.int32, (1, PICKED), 1).astype(FULL)
        lane_image = jnp.where(lane < IMAGES, lane, lane - IMAGES)
        lane_place = jnp.where(lane < IMAGES, float(TABLE), TABLE + 1.0)
        back_pick = (
            (image_col == lane_image) & (place_col == lane_place) & (lane < 2.0 * IMAGES)
        ).astype(LOW)
        back = dot(jnp.concatenate([back_pick] * 3, axis=1), back_parts)
        grad = back[:, :D] + dot_nt(kv[r, :], wqkv[1, :, D:])
        unit = unit_c[r, :]
        dx[r, :] = back[:, D:] + norm_back(grad, vec(1, 0), unit, inv_c[r, 0:1])
        return gain_sum + col_sum(grad * unit), bias_sum + col_sum(grad)

    zero_row = jnp.zeros((1, D), FULL)
    gain_sum, bias_sum = rolled(SEQ // ROWS, kv_back, (zero_row, zero_row), 1.1)
    put_row(PRE_GAIN_AT, gain_sum)
    put_row(PRE_BIAS_AT, bias_sum)
    flat[LAYER_END:, :] = jnp.zeros((LAYER_ALL - LAYER_END, LANES), FULL)
    gather_rows(b1, layer_rows)
    plan.spend(1.5)
    scatter_1.start(0)

    def feed_back(i, carry):
        fc1_sum, fc2_sum, proj_sum, gain_sum, bias_sum = carry
        r = tile_rows(i)
        grad_out = dx[r, :]
        out_low = grad_out.astype(LOW)
        low[r, :] = out_low
        for c in range(4):
            lanes = slice(c * D, (c + 1) * D)
            slope[r, lanes] = (dot_nt(out_low, wfc2[0, lanes, :]) * slope[r, lanes].astype(FULL)).astype(LOW)
        grad_h = dot_nt(slope[r, :], wfc1[0])
        unit = unit_b[r, :]
        middle = grad_out + norm_back(grad_h, vec(0, 5), unit, inv_b[r, 0:1])
        dx[r, :] = middle
        middle_low = middle.astype(LOW)
        h2low[r, :] = middle_low
        gatt[r, :] = dot_nt(middle_low, wproj[0]).astype(LOW)
        return (
            fc1_sum + col_sum(slope[r, :]), fc2_sum + col_sum(out_low), proj_sum + col_sum(middle_low),
            gain_sum + col_sum(grad_h * unit), bias_sum + col_sum(grad_h),
        )

    h2low = kv.at[:, 0:D]
    gatt = kv.at[:, D : 2 * D]
    sums = rolled(SEQ // ROWS, feed_back, (jnp.zeros((1, FF), FULL),) + (zero_row,) * 4, 4.5)
    for at, value in zip((FC1_BIAS_AT, FC2_BIAS_AT, PROJ_BIAS_AT, MID_GAIN_AT, MID_BIAS_AT), sums):
        put_row(at, value)


    def feed_weights(c, carry):
        lanes = pl.ds(pl.multiple_of(c * D, D), D)
        put(FC2_AT, c * D, D, dot_tn(act[:, lanes], low[...]))
        put(FC1_AT, 0, FF, dot_tn(h_b[...], slope[:, lanes]), 3 * c)
        return carry

    rolled(4, feed_weights, None, 2.0)
    put(PROJ_AT, 0, D, dot_tn(attl[...], h2low[...]))
    flat[LAYER_END:, :] = jnp.zeros((LAYER_ALL - LAYER_END, LANES), FULL)
    gather_rows(b0, layer_rows, first_early)
    plan.spend(1.6)
    scatter_0.start(0)

    def attend_back(j, carry):
        r = window_rows(j)
        mine, _ = window_masks(j, r)
        for g in range(HEADS // 2):
            lanes = slice(g * LANES, (g + 1) * LANES)
            key_lanes = slice(D + g * LANES, D + (g + 1) * LANES)
            value_lanes = slice(2 * D + g * LANES, 2 * D + (g + 1) * LANES)
            q2 = both(qkv[r, lanes])
            go2 = both(gatt[r, lanes])
            keys = qkv[r, key_lanes]
            p_low = probs[j, g]
            p = p_low.astype(FULL)
            gp = dot_nt(qkv[r, value_lanes], go2)
            gs = (p * (gp - jnp.sum(p * gp, axis=0, keepdims=True))).astype(LOW)
            keep_own(mine, qkv, r, lanes, merge(dot_tn(gs, keys)) * SCORE_SCALE)
            keep_own(mine, qkv, r, key_lanes, dot(gs, q2) * SCORE_SCALE)
            keep_own(mine, qkv, r, value_lanes, dot(p_low, go2))
        return carry

    loop(WINDOWS, attend_back, None, 0.7)

    def qkv_cast(i, carry):
        query_sum, value_sum = carry
        r = tile_rows(i)
        held = seg_col[r, 0:1] < float(IMAGES)
        grads = jnp.where(held, qkv[r, :].astype(FULL), 0.0)
        qkv[r, :] = grads.astype(LOW)
        return query_sum + col_sum(grads[:, :D]), value_sum + col_sum(grads[:, 2 * D :])

    query_sum, value_sum = rolled(SEQ // ROWS, qkv_cast, (zero_row, zero_row), 0.5)
    put_row(QUERY_BIAS_AT, query_sum)
    put_row(VALUE_BIAS_AT, value_sum)

    def qkv_weights(c, carry):
        put(QKV_AT, 0, 3 * D, dot_tn(h_a[...], qkv[:, pl.ds(pl.multiple_of(c * D, D), D)]), 3 * c)
        return carry

    lax.fori_loop(0, 3, qkv_weights, 0)
    gather_rows(b0, layer_rows, 0, first_early)
    plan.spend(1.2)
    scatter_0.start(1)

    def qkv_back(i, carry):
        gain_sum, bias_sum, embed_sum = carry
        r = tile_rows(i)
        grad = dot_nt(qkv[r, :], wqkv[0])
        unit = unit_a[r, :]
        full = dx[r, :] + norm_back(grad, vec(0, 0), unit, inv_a[r, 0:1])
        dx[r, :] = full
        place = pos_col[r, 0:1]
        pixel = jnp.where(place < TABLE, full, 0.0).astype(LOW)
        low[r, :] = pixel
        return gain_sum + col_sum(grad * unit), bias_sum + col_sum(grad), embed_sum + col_sum(pixel)

    gain_sum, bias_sum, embed_sum = rolled(SEQ // ROWS, qkv_back, (zero_row,) * 3, 2.1)
    put_row(PRE_GAIN_AT, gain_sum)
    put_row(PRE_BIAS_AT, bias_sum)
    gather_rows(b0, layer_rows, *vector_blocks)
    plan.spend(0.1)
    scatter_0.start(2)

    for c in range(2):
        put(PATCH_AT, c * D, D, dot_tn(pat[:, c * D : (c + 1) * D], low[...]))
    place_col = pos_col[:, 0:1]
    onehot = onehot_of(place_col)
    high = dx[...].astype(LOW)
    rest = (dx[...] - high.astype(FULL)).astype(LOW)
    table = dot_tn(onehot, high) + dot_tn(onehot, rest)
    put(POS_AT, 0, D, table[: TABLE + 2])
    put_row(PATCH_BIAS_AT, embed_sum)
    flat[FINAL_GAIN_AT : FINAL_GAIN_AT + kept, :] = edge[:kept, :]
    gather_rows(bg, global_rows, 0, border + 1)
    plan.spend(1.5)
    scatter_g.start(1)
    plan.until()

    squares = jnp.zeros((1, 1), FULL)
    for ref in (new_l, new_g):
        used = ref[...]
        squares += jnp.sum(jnp.sum(used * used, axis=0, keepdims=True), axis=1, keepdims=True)
    row = lax.broadcasted_iota(jnp.int32, (8, LANES), 0)
    tile = jnp.where(row == 0, squares, loss_sum)
    shared[...] = add_over_slice(place, tile, tiles, tile_send, tile_recv)
    for scatter in scatters:
        scatter.drain()


def padded(rows):
    return rows + -rows % 16


def step_call(place, loss_scale, pat, pos, seg, lab, tea, lm, gm):
    vmem = pl.BlockSpec(memory_space=pltpu.VMEM)
    smem = pl.BlockSpec(memory_space=pltpu.SMEM)
    n, nz = place.n, place.nz
    rows = padded(lm.shape[0] // 2), padded(lm.shape[0] // 2), padded(gm.shape[0])

    def shape(*dims, kind=FULL):
        return pltpu.VMEM(dims, kind)

    def low(*dims):
        return pltpu.VMEM(dims, LOW)

    scratch = [low(n, 2, nz, n, r, LANES) for r in rows]
    for r in rows:
        scratch += [
            low(n, nz, n, r, LANES), low(n - 1, n, nz, r, LANES), low(n - 1, nz, r, LANES), low(nz - 1, r, LANES)
        ]
    tiles = 2 * nz + n * n
    scratch += [
        shape(LAYER_ALL, LANES), shape(gm.shape[0] + 8, LANES), shape(rows[0], LANES), low(D, GROUP * LANES),
        low(2, D, 3 * D), low(2, D, D), low(2, D, FF), low(2, FF, D),
        low(PATCH, D), low(256, D), low(GROUPS, (GROUP_ROWS + 1) * LANES),
        shape(2, 16, FF),
        shape(SEQ, LANES), shape(SEQ, LANES),
        shape(SEQ, D), shape(SEQ, LANES), low(SEQ, D),
        shape(SEQ, D), shape(SEQ, LANES), low(SEQ, D),
        low(SEQ, 3 * D), low(WINDOWS, HEADS // 2, WINDOW, 2 * WINDOW),
        low(SEQ, D), shape(SEQ, D), shape(SEQ, D),
        low(SEQ, FF), low(SEQ, FF), low(SEQ, 2 * D), low(SEQ, D), shape(SEQ, LANES),
        shape(tiles, 8, LANES),
        pltpu.SemaphoreType.DMA((6,)),
        pltpu.SemaphoreType.DMA((3, nz + nz * n + 2 * n)), pltpu.SemaphoreType.DMA((3, 2 * n * n * nz + n * nz + nz)),
        pltpu.SemaphoreType.DMA((2,)), pltpu.SemaphoreType.DMA((2,)),
    ]
    return pl.pallas_call(
        functools.partial(step_kernel, place, loss_scale),
        out_shape=[jax.ShapeDtypeStruct(a, FULL) for a in (lm.shape, gm.shape, (8, LANES))],
        in_specs=[vmem] * 3 + [smem] * 2 + [vmem] * 2,
        out_specs=[vmem] * 3,
        scratch_shapes=scratch,
        compiler_params=pltpu.CompilerParams(collective_id=0, has_side_effects=True, vmem_limit_bytes=VMEM_BYTES),
    )(pat, pos, seg, lab, tea, lm, gm)

def adam_kernel(total, gl, gg, lm, lo, ls, gm, go, gs, *outs):
    norm = jnp.sqrt(total[0:1, 0:1])
    factor = jnp.minimum(1.0, CLIP_NORM / norm)
    fix_one = 1.0 - BETA_ONE**STEP
    fix_two = 1.0 - BETA_TWO**STEP
    for at, (grad, master, moment, second) in ((0, (gl, lm, lo, ls)), (3, (gg, gm, go, gs))):
        clipped = grad[...] * factor
        new_moment = BETA_ONE * moment[...] + (1.0 - BETA_ONE) * clipped
        new_second = BETA_TWO * second[...] + (1.0 - BETA_TWO) * clipped * clipped
        old = master[...]
        update = new_moment / fix_one / (jnp.sqrt(new_second / fix_two) + ADAM_EPS) + WEIGHT_DECAY * old
        outs[at][...] = old - LEARN_RATE * update
        outs[at + 1][...] = new_moment
        outs[at + 2][...] = new_second
    outs[6][0, 0] = norm[0, 0]
    outs[7][0, 0] = total[1, 0]


def interleave(x):
    rows = x.shape[1] // LANES
    return x.reshape(2, rows, LANES).transpose(1, 0, 2).reshape(2 * rows, LANES)


def layers_apart(x):
    rows = x.shape[0] // 2
    return x.reshape(rows, 2, LANES).transpose(1, 0, 2).reshape(2, rows * LANES)


def shards(sizes, pat, pos, seg, lab, tea, lm, lo, ls, gm, go, gs):
    place = Place(sizes)
    count = sizes[0] * sizes[1]
    assert pat.shape[0] == 1 and lm.shape[1] * count == LAYER_ALL * LANES and gm.shape[0] * count == GLOBAL_ALL * LANES
    lm, lo, ls = interleave(lm), interleave(lo), interleave(ls)
    gm, go, gs = gm.reshape(-1, LANES), go.reshape(-1, LANES), gs.reshape(-1, LANES)
    gl, gg, total = step_call(place, 1.0 / (2 * IMAGES * count), pat[0], pos, seg, lab, tea, lm, gm)
    vmem, smem = pl.BlockSpec(memory_space=pltpu.VMEM), pl.BlockSpec(memory_space=pltpu.SMEM)
    shapes = [lm.shape] * 3 + [gm.shape] * 3 + [(1, 1)] * 2
    *new, norm, loss = pl.pallas_call(
        adam_kernel,
        out_shape=[jax.ShapeDtypeStruct(x, FULL) for x in shapes],
        out_specs=[vmem] * 6 + [smem] * 2,
        compiler_params=pltpu.CompilerParams(vmem_limit_bytes=VMEM_BYTES),
    )(total, gl, gg, lm, lo, ls, gm, go, gs)
    return tuple(layers_apart(x) for x in new[:3]) + tuple(x.reshape(-1) for x in new[3:]) + (norm.reshape(()), loss.reshape(()))


def solution(mesh):
    axes = tuple(mesh.axis_names)
    split = P(axes)
    wide = P(None, axes)
    return jax.shard_map(
        functools.partial(shards, tuple(mesh.shape[a] for a in axes)),
        mesh=mesh,
        in_specs=(split,) * 5 + (wide,) * 3 + (split,) * 3,
        out_specs=(wide,) * 3 + (split,) * 3 + (P(), P()),
        check_vma=False,
    )
```

profile of v0, /device:TPU:0, one launch (start us, length us, event | category | flops | bytes accessed | tf_op | source)
XLA Modules:
  0.0 145.4 jit_solution(13957334755345591458)
XLA Ops:
  0.6 141.3 %shard_map.170 = (f32[880,128]{1,0:T(8,128)}, f32[280,128]{1,0:T(8,128)}, f32[8,128]{1,0:T(8,128)}) custom-call(bf16[768,768]{1,0:T(8,128)(2,1)} %bitcast.41, s32[1,768]{1,0:T(1,128)} %pos.1, s32[1,768]{1,0:T(1,128)} %seg.1, s32[1,15]{1,0:T(1,128)} %lab.1, s32[1,15]{1,0:T(1,128)} %tea.1, f32[880,128]{1,0:T(8,128)} %bitcast.39, f32[280,128]{1,0:T(8,128)} %bitcast.42), custom_call_target="tpu_custom_call" | custom-call | tf_op jit(solution)/shard_map/pallas_call | solution.py:1092
  141.9 3.3 %shard_map.171 = (f32[880,128]{1,0:T(8,128)}, f32[880,128]{1,0:T(8,128)}, f32[880,128]{1,0:T(8,128)}, f32[280,128]{1,0:T(8,128)}, f32[280,128]{1,0:T(8,128)}, /*...) custom-call(f32[8,128]{1,0:T(8,128)} %get-tuple-element.19.total, f32[880,128]{1,0:T(8,128)} %get-tuple-element.20.gl, ...), custom_call_target="tpu_custom_call" | custom-call | tf_op jit(solution)/shard_map/pallas_call | solution.py:1138
where the time goes:
time: 146 us; the launch traced here: 145 us
  Pallas kernels  145 us (99%)
    pallas_call x1, Pallas kernels, step_call(): pl.pallas_call(functools.partial(step_kernel, place, loss_scale), out_sha...  141 us
    pallas_call x1, Pallas kernels, shards(): pl.pallas_call(adam_kernel, out_shape=[jax.ShapeDtypeStruct(x, FULL) for...  3.27 us

commit v1 on v0

--- a/solution.py
+++ b/solution.py
@@ -42,7 +42,7 @@
 HEAD_LANES = 2048
 PICKED = 32
 WINDOWS, WINDOW = 8, 128
-ROWS = 256
+ROWS = 384
 LAYER_ALL, GLOBAL_ALL = 14080, 8960
 VMEM_BYTES = 64 * 1024 * 1024 - 64 * 1024
 MESH = pl.DeviceIdType.MESH
@@ -82,15 +82,14 @@
 
 
 def gelu_parts(x):
-    size = jnp.abs(x)
-    bell = jnp.exp(-0.5 * x * x)
-    base = 1.0 + (0.3275911 * 0.7071067811865476) * size
+    bell = jnp.exp2(x * x * (-0.5 * 1.4426950408889634))
+    base = 1.0 + (0.3275911 * 0.7071067811865476) * jnp.abs(x)
     t = pl.reciprocal(base, approx=True)
     t = t * (2.0 - base * t)
-    tail = ((((1.061405429 * t - 1.453152027) * t + 1.421413741) * t - 0.284496736) * t + 0.254829592) * t
-    tail = 0.5 * tail * bell
+    tail = (((0.5307027145 * t - 0.7265760135) * t + 0.7107068705) * t - 0.142248368) * t + 0.127414796
+    tail = tail * t * bell
     phi = jnp.where(x < 0, tail, 1.0 - tail)
-    return x * phi, phi + x * (bell * 0.3989422804014327)
+    return x * phi, phi + x * bell * 0.3989422804014327
 
 
 def exact_parts(x):
@@ -193,10 +192,13 @@
     def spend(self, time):
         self.now += time
         while True:
-            step = next((step for step in self.steps if self.ready(step) <= self.now), None)
+            step = min((step for step in self.steps if self.ready(step) <= self.now), key=self.ready, default=None)
             if step is None:
                 return
             self.run(step)
+
+    def due(self, time):
+        return any(self.ready(step) <= self.now + time for step in self.steps)
 
     def until(self, name=None):
         while self.steps and (name is None or any(step[2] == name for step in self.steps)):
@@ -462,16 +464,18 @@
 
 def step_kernel(
     place, loss_scale,
-    pat, pos, seg, lab, tea, lm, gm,
+    pat_hbm, pos, seg, lab, tea, lm, gm,
     new_l, new_g, shared,
     b0, b1, bg, r0c, r0q, r0p, r0z, r1c, r1q, r1p, r1z, rgc, rgq, rgp, rgz, flat, edge, stage, arrange,
     wqkv, wproj, wfc1, wfc2, wpat, wpos, whead, vecs,
     pos_col, seg_col, unit_a, inv_a, h_a, unit_b, inv_b, h_b, qkv, probs, attl, x0, x1, slope, act, kv, low, inv_c,
-    tiles, sends, gather_recv, scatter_recv, tile_send, tile_recv,
+    pat, pat_sem, tiles, sends, gather_recv, scatter_recv, tile_send, tile_recv,
 ):
     layer_rows, global_rows = lm.shape[0] // 2, gm.shape[0]
     place.locate()
     me = place.block(0, 0, 0)
+    pat_load = pltpu.make_async_copy(pat_hbm, pat, pat_sem)
+    pat_load.start()
     bg[me + (pl.ds(0, global_rows),)] = gm[...].astype(LOW)
     b0[me + (pl.ds(0, layer_rows),)] = lm[pl.ds(0, layer_rows, stride=2), :].astype(LOW)
     b1[me + (pl.ds(0, layer_rows),)] = lm[pl.ds(1, layer_rows, stride=2), :].astype(LOW)
@@ -507,9 +511,9 @@
         return (s < -(-FINAL_GAIN_AT // global_rows)).astype(jnp.int32)
 
     scatter_g = Scatter(place, plan, bg, rgc, rgq, rgp, rgz, finish_global, sends.at[5], scatter_recv.at[2],
-                        (0.7, 0.5), global_turn)
+                        (0.65, 0.4), global_turn)
     scatter_0 = Scatter(place, plan, b0, r0c, r0q, r0p, r0z, finish_layer(0), sends.at[4], scatter_recv.at[1],
-                        (0.9, 0.5, 0.05), layer_turn)
+                        (0.75, 0.35, 0.03), layer_turn)
     scatter_1 = Scatter(place, plan, b1, r1c, r1q, r1p, r1z, finish_layer(1), sends.at[3], scatter_recv.at[0],
                         (1.0,), lambda s: 0 * s)
     scatters = [scatter_g, scatter_0, scatter_1]
@@ -525,9 +529,20 @@
         return carry
 
     def rolled(count, body, carry=None, time=0.0):
-        carry = lax.fori_loop(0, count, body, 0 if carry is None else carry)
-        plan.spend(time)
-        return carry
+        traced = []
+
+        def one(i, carry):
+            assert not traced
+            traced.append(i)
+            carry = body(i, carry)
+            for k in range(count):
+                if plan.due(time):
+                    pl.when(i == k)(lambda: plan.spend(time))
+                else:
+                    plan.spend(time)
+            return carry
+
+        return lax.fori_loop(0, count, one, 0 if carry is None else carry)
 
     def each_block(low_end, high_end, one):
         def body(s, carry):
@@ -669,7 +684,8 @@
         inv_a[r, :] = jnp.broadcast_to(inverse, (ROWS, LANES))
         return carry
 
-    rolled(SEQ // ROWS, embed, None, 1.8)
+    pat_load.wait()
+    rolled(SEQ // ROWS, embed, None, 0.9)
     plan.until(1)
     take_layer(0, b0)
     plan.spend(1.8)
@@ -682,7 +698,7 @@
         qkv[r, :] = (dot(h, wqkv[0]) + qkv_bias).astype(LOW)
         return carry
 
-    rolled(SEQ // ROWS, project, None, 1.2)
+    rolled(SEQ // ROWS, project, None, 0.6)
 
     def window_rows(j):
         return pl.ds(min(102 * j // 16 * 16, SEQ - WINDOW), WINDOW)
@@ -740,7 +756,7 @@
         x1[r, :] = middle + dot(act[r, :], wfc2[0]) + vec(0, 8)
         return carry
 
-    rolled(SEQ // ROWS, feed, None, 8.0)
+    rolled(SEQ // ROWS, feed, None, 4.0)
 
     plan.until(2)
     take_layer(1, b1)
@@ -759,7 +775,7 @@
         kv[r, :] = (dot(h, wqkv[1, :, D:]) + bias).astype(LOW)
         return carry
 
-    rolled(SEQ // ROWS, kv_rows, None, 1.2)
+    rolled(SEQ // ROWS, kv_rows, None, 0.6)
 
     h_s = dot(picker_low, h_c[...]).astype(LOW)
     x_s = sum(dot(picker_low, part) for part in exact_parts(x1[...]))
@@ -915,7 +931,7 @@
         return gain_sum + col_sum(grad * unit), bias_sum + col_sum(grad)
 
     zero_row = jnp.zeros((1, D), FULL)
-    gain_sum, bias_sum = rolled(SEQ // ROWS, kv_back, (zero_row, zero_row), 1.1)
+    gain_sum, bias_sum = rolled(SEQ // ROWS, kv_back, (zero_row, zero_row), 0.4)
     put_row(PRE_GAIN_AT, gain_sum)
     put_row(PRE_BIAS_AT, bias_sum)
     flat[LAYER_END:, :] = jnp.zeros((LAYER_ALL - LAYER_END, LANES), FULL)
@@ -946,7 +962,7 @@
 
     h2low = kv.at[:, 0:D]
     gatt = kv.at[:, D : 2 * D]
-    sums = rolled(SEQ // ROWS, feed_back, (jnp.zeros((1, FF), FULL),) + (zero_row,) * 4, 4.5)
+    sums = rolled(SEQ // ROWS, feed_back, (jnp.zeros((1, FF), FULL),) + (zero_row,) * 4, 2.3)
     for at, value in zip((FC1_BIAS_AT, FC2_BIAS_AT, PROJ_BIAS_AT, MID_GAIN_AT, MID_BIAS_AT), sums):
         put_row(at, value)
 
@@ -957,7 +973,7 @@
         put(FC1_AT, 0, FF, dot_tn(h_b[...], slope[:, lanes]), 3 * c)
         return carry
 
-    rolled(4, feed_weights, None, 2.0)
+    rolled(4, feed_weights, None, 0.5)
     put(PROJ_AT, 0, D, dot_tn(attl[...], h2low[...]))
     flat[LAYER_END:, :] = jnp.zeros((LAYER_ALL - LAYER_END, LANES), FULL)
     gather_rows(b0, layer_rows, first_early)
@@ -993,7 +1009,7 @@
         qkv[r, :] = grads.astype(LOW)
         return query_sum + col_sum(grads[:, :D]), value_sum + col_sum(grads[:, 2 * D :])
 
-    query_sum, value_sum = rolled(SEQ // ROWS, qkv_cast, (zero_row, zero_row), 0.5)
+    query_sum, value_sum = rolled(SEQ // ROWS, qkv_cast, (zero_row, zero_row), 0.2)
     put_row(QUERY_BIAS_AT, query_sum)
     put_row(VALUE_BIAS_AT, value_sum)
 
@@ -1018,7 +1034,7 @@
         low[r, :] = pixel
         return gain_sum + col_sum(grad * unit), bias_sum + col_sum(grad), embed_sum + col_sum(pixel)
 
-    gain_sum, bias_sum, embed_sum = rolled(SEQ // ROWS, qkv_back, (zero_row,) * 3, 2.1)
+    gain_sum, bias_sum, embed_sum = rolled(SEQ // ROWS, qkv_back, (zero_row,) * 3, 1.0)
     put_row(PRE_GAIN_AT, gain_sum)
     put_row(PRE_BIAS_AT, bias_sum)
     gather_rows(b0, layer_rows, *vector_blocks)
@@ -1084,7 +1100,7 @@
         low(SEQ, 3 * D), low(WINDOWS, HEADS // 2, WINDOW, 2 * WINDOW),
         low(SEQ, D), shape(SEQ, D), shape(SEQ, D),
         low(SEQ, FF), low(SEQ, FF), low(SEQ, 2 * D), low(SEQ, D), shape(SEQ, LANES),
-        shape(tiles, 8, LANES),
+        low(SEQ, PATCH), pltpu.SemaphoreType.DMA, shape(tiles, 8, LANES),
         pltpu.SemaphoreType.DMA((6,)),
         pltpu.SemaphoreType.DMA((3, nz + nz * n + 2 * n)), pltpu.SemaphoreType.DMA((3, 2 * n * n * nz + n * nz + nz)),
         pltpu.SemaphoreType.DMA((2,)), pltpu.SemaphoreType.DMA((2,)),
@@ -1092,7 +1108,7 @@
     return pl.pallas_call(
         functools.partial(step_kernel, place, loss_scale),
         out_shape=[jax.ShapeDtypeStruct(a, FULL) for a in (lm.shape, gm.shape, (8, LANES))],
-        in_specs=[vmem] * 3 + [smem] * 2 + [vmem] * 2,
+        in_specs=[pl.BlockSpec(memory_space=pl.ANY)] + [vmem] * 2 + [smem] * 2 + [vmem] * 2,
         out_specs=[vmem] * 3,
         scratch_shapes=scratch,
         compiler_params=pltpu.CompilerParams(collective_id=0, has_side_effects=True, vmem_limit_bytes=VMEM_BYTES),

time: 146 us -> 140 us (0.959)
  Pallas kernels: 145 us -> 139 us
    pallas_call x1, Pallas kernels: 141 us -> 135 us  [step_call(): pl.pallas_call(functools.partial(step_kernel, place, loss_scale), out_sha...]
where the time goes in v1:
time: 140 us; the launch traced here: 139 us
  Pallas kernels  139 us (99%)
    pallas_call x1, Pallas kernels, step_call(): pl.pallas_call(functools.partial(step_kernel, place, loss_scale), out_sha...  135 us
    pallas_call x1, Pallas kernels, shards(): pl.pallas_call(adam_kernel, out_shape=[jax.ShapeDtypeStruct(x, FULL) for...  3.27 us

profile of v1, /device:TPU:0, one launch (start us, length us, event | category | flops | bytes accessed | tf_op | source)
XLA Modules:
  0.0 139.3 jit_solution(14421941502405100460)
XLA Ops:
  0.6 135.3 %shard_map.170 = (f32[880,128]{1,0:T(8,128)}, f32[280,128]{1,0:T(8,128)}, f32[8,128]{1,0:T(8,128)}) custom-call(bf16[768,768]{1,0:T(8,128)(2,1)} %bitcast.41, s32[1,768]{1,0:T(1,128)} %pos.1, s32[1,768]{1,0:T(1,128)} %seg.1, s32[1,15]{1,0:T(1,128)} %lab.1, s32[1,15]{1,0:T(1,128)} %tea.1, f32[880,128]{1,0:T(8,128)} %bitcast.39, f32[280,128]{1,0:T(8,128)} %bitcast.42), custom_call_target="tpu_custom_call" | custom-call | tf_op jit(solution)/shard_map/pallas_call | solution.py:1108
  135.9 3.3 %shard_map.171 = (f32[880,128]{1,0:T(8,128)}, f32[880,128]{1,0:T(8,128)}, f32[880,128]{1,0:T(8,128)}, f32[280,128]{1,0:T(8,128)}, f32[280,128]{1,0:T(8,128)}, /*...) custom-call(f32[8,128]{1,0:T(8,128)} %get-tuple-element.19.total, f32[880,128]{1,0:T(8,128)} %get-tuple-element.20.gl, ...), custom_call_target="tpu_custom_call" | custom-call | tf_op jit(solution)/shard_map/pallas_call | solution.py:1154

commit v2 on v1

--- a/solution.py
+++ b/solution.py
@@ -167,7 +167,7 @@
 
 
 class Plan:
-    HOP = 2.5
+    HOP = 2.0
     RATES = (88e3, 66e3, 600e3)
 
     def __init__(self):

time: 140 us -> 138 us (0.986)
  Pallas kernels: 139 us -> 137 us
where the time goes in v2:
time: 138 us
  Pallas kernels  137 us (99%)
    pallas_call x1, Pallas kernels, step_call(): pl.pallas_call(functools.partial(step_kernel, place, loss_scale), out_sha...  134 us
    pallas_call x1, Pallas kernels, shards(): pl.pallas_call(adam_kernel, out_shape=[jax.ShapeDtypeStruct(x, FULL) for...  3.27 us

profile of v2, /device:TPU:0, one launch (start us, length us, event | category | flops | bytes accessed | tf_op | source)
XLA Modules:
  0.0 138.0 jit_solution(421104017703211373)
XLA Ops:
  0.6 133.9 %shard_map.170 = (f32[880,128]{1,0:T(8,128)}, f32[280,128]{1,0:T(8,128)}, f32[8,128]{1,0:T(8,128)}) custom-call(bf16[768,768]{1,0:T(8,128)(2,1)} %bitcast.41, s32[1,768]{1,0:T(1,128)} %pos.1, s32[1,768]{1,0:T(1,128)} %seg.1, s32[1,15]{1,0:T(1,128)} %lab.1, s32[1,15]{1,0:T(1,128)} %tea.1, f32[880,128]{1,0:T(8,128)} %bitcast.39, f32[280,128]{1,0:T(8,128)} %bitcast.42), custom_call_target="tpu_custom_call" | custom-call | tf_op jit(solution)/shard_map/pallas_call | solution.py:1108
  134.6 3.3 %shard_map.171 = (f32[880,128]{1,0:T(8,128)}, f32[880,128]{1,0:T(8,128)}, f32[880,128]{1,0:T(8,128)}, f32[280,128]{1,0:T(8,128)}, f32[280,128]{1,0:T(8,128)}, /*...) custom-call(f32[8,128]{1,0:T(8,128)} %get-tuple-element.19.total, f32[880,128]{1,0:T(8,128)} %get-tuple-element.20.gl, ...), custom_call_target="tpu_custom_call" | custom-call | tf_op jit(solution)/shard_map/pallas_call | solution.py:1154
